TPU v7x, 256 devices: a whole 4x4x8 slice. The times are simulated.
256 devices in a mesh: head: 4 (over x), ctx: 64 (over z, y, core).
Axes of the slice: x: 4, y: 4, z: 8, core: 2. Of those that a mesh axis runs over, the one named last changes fastest.
Arguments:
- query: bfloat16 [256, 384, 3072], P('ctx', 'head'), may hold values from -6 to 6
- keys_in: bfloat16 [256, 384, 3072], P('ctx', 'head'), may hold values from -6 to 6
- values_in: bfloat16 [256, 384, 3072], P('ctx', 'head'), may hold values from -6 to 6
- pair_keys: int32 [256, 8], P('ctx'), may hold values from 0 to 255, as said below
- pair_count: int32 [256], P('ctx'), may hold values from 1 to 8
Outputs:
- attended: bfloat16 [256, 384, 3072], P('ctx', 'head')
Inputs may be any that keep to these rules, and one draw needn't show every extreme that they name: `pair_keys`: entry 0 of row t is t itself; entries 0 to pair_count[t] - 1 are distinct; every entry of row t, used or not, names a tile whose ctx index differs from that of t by at most 1; entries from pair_count[t] on are ignored.
All inputs are finite; a program needn't handle non-finite values.
Results may differ from a plain program's by a relative error of at most 0.0045.
Values may be sent and summed in bfloat16 or wider, within the bound.
A program may use at most 128 MiB of HBM per device.

v0:
```python
import jax
import jax.numpy as jnp
from jax import lax
from jax.sharding import PartitionSpec as P

DH = 128
REACH = 1
MOST = 8


def extended(block, sides, width):
    for axis, dim in sides:
        count = lax.axis_size(axis)
        forward = [(i, i + 1) for i in range(count - 1)]
        backward = [(target, source) for source, target in forward]
        low = lax.ppermute(
            lax.slice_in_dim(block, block.shape[dim] - width, None, axis=dim), axis, forward
        )
        high = lax.ppermute(lax.slice_in_dim(block, 0, width, axis=dim), axis, backward)
        block = jnp.concatenate([low, block, high], axis=dim)
    return block


def attend(carry_state, query_tile, kv_tile, is_pair):

    def update(old_state):
        run_max, run_sum, run_out = old_state
        keys_tile = kv_tile[0].reshape(kv_tile.shape[1], -1, DH)
        values_tile = kv_tile[1].reshape(kv_tile.shape[1], -1, DH)
        scores = jnp.einsum(
            "qhd,khd->qhk", query_tile, keys_tile, preferred_element_type=jnp.float32
        ) * DH ** (-0.5)
        tile_max = jnp.max(scores, axis=-1)
        expo = jnp.exp(scores - tile_max[..., None])
        tile_sum = jnp.sum(expo, axis=-1)
        weights = expo.astype(jnp.bfloat16)
        tile_out = jnp.einsum(
            "qhk,khd->qhd", weights, values_tile, preferred_element_type=jnp.float32
        )
        new_max = jnp.maximum(run_max, tile_max)
        old_factor = jnp.exp(run_max - new_max)
        new_factor = jnp.exp(tile_max - new_max)
        return (
            new_max,
            run_sum * old_factor + tile_sum * new_factor,
            run_out * old_factor[..., None] + tile_out * new_factor[..., None],
        )

    return lax.cond(is_pair, update, lambda old_state: old_state, carry_state)


def finish(carry_state):
    run_max, run_sum, run_out = carry_state
    merged = run_out / run_sum[..., None]
    return merged.reshape(merged.shape[0], -1).astype(jnp.bfloat16)


def body(query, keys_in, values_in, pair_keys, pair_count):
    tiles_dev = query.shape[0]
    q_heads, k_heads, v_heads = (
        lax.all_to_all(query, "head", split_axis=2, concat_axis=1, tiled=True),
        lax.all_to_all(keys_in, "head", split_axis=2, concat_axis=1, tiled=True),
        lax.all_to_all(values_in, "head", split_axis=2, concat_axis=1, tiled=True),
    )
    tile_rows = q_heads.shape[1]
    heads_dev = q_heads.shape[2] // DH
    pairs_kv = jnp.stack([k_heads, v_heads])
    first_slot = lax.axis_index("ctx") * tiles_dev
    margin = REACH * tiles_dev
    empty_state = (
        jnp.full((tile_rows, heads_dev), -1e30, jnp.float32),
        jnp.zeros((tile_rows, heads_dev), jnp.float32),
        jnp.zeros((tile_rows, heads_dev, DH), jnp.float32),
    )
    window = extended(pairs_kv, (("ctx", 1),), margin)

    def per_tile(t):
        query_tile = q_heads[t].reshape(tile_rows, heads_dev, DH)
        listed_keys = pair_keys[t]
        live_count = pair_count[t]

        def advance(p, carry_state):
            key_slot = listed_keys[p] - first_slot + margin
            kv_tile = lax.dynamic_index_in_dim(window, key_slot, 1, keepdims=False)
            return attend(carry_state, query_tile, kv_tile, p < live_count)

        return finish(lax.fori_loop(0, MOST, advance, empty_state))

    outputs = lax.map(per_tile, jnp.arange(tiles_dev))
    return lax.all_to_all(outputs, "head", split_axis=1, concat_axis=2, tiled=True)


def solution(mesh):
    in_specs = (
        P("ctx", "head", None),
        P("ctx", "head", None),
        P("ctx", "head", None),
        P("ctx", None),
        P("ctx"),
    )
    out_specs = P("ctx", "head", None)
    return jax.shard_map(body, mesh=mesh, in_specs=in_specs, out_specs=out_specs, check_vma=False)
```

profile of v0, /device:TPU:88, one launch (start us, length us, event | category | flops | bytes accessed | tf_op | source)
XLA Modules:
  0.0 419.8 jit_solution(176157566797071298)
XLA Ops:
  0.0 5.7 %copy.49 = bf16[4,96,3072]{1,0,2:T(4,128)(2,1)} copy(bf16[4,96,3072]{2,1,0:T(8,128)(2,1)} %param.12) | data formatting | bytes 4718592 | tf_op args[1]
  10.0 5.7 %copy.52 = bf16[4,96,3072]{1,0,2:T(4,128)(2,1)} copy(bf16[4,96,3072]{2,1,0:T(8,128)(2,1)} %param.13) | data formatting | bytes 4718592 | tf_op args[2]
  15.6 31.9 %all-to-all-done.1 = bf16[4,96,3072]{1,0,2:T(4,128)(2,1)S(1)} async-done(((bf16[4,96,3072]{1,0,2:T(4,128)(2,1)}), bf16[4,96,3072]{1,0,2:T(4,128)(2,1)S(1)}, u32[]{:S(2)}, u32[]{:S(2)}) %all-to-all-start.1) | async-done | bytes 2359328 | tf_op jit(solution)/shard_map/all_to_all | solution.py:62
  58.3 32.4 %all-to-all-done.2 = bf16[4,96,3072]{1,0,2:T(4,128)(2,1)} async-done(((bf16[4,96,3072]{1,0,2:T(4,128)(2,1)}), bf16[4,96,3072]{1,0,2:T(4,128)(2,1)}, u32[]{:S(2)}, u32[]{:S(2)}) %all-to-all-start.2) | async-done | bytes 2359328 | tf_op jit(solution)/shard_map/all_to_all | solution.py:63
  90.7 5.7 %copy.54 = bf16[4,4,96,768]{3,2,1,0:T(8,128)(2,1)} copy(bf16[4,4,96,768]{2,0,3,1:T(4,128)(2,1)} %bitcast.20) | data formatting | bytes 4718592 | tf_op jit(solution)/shard_map/all_to_all | solution.py:63
  106.2 5.7 %copy.46 = bf16[4,96,3072]{1,0,2:T(4,128)(2,1)} copy(bf16[4,96,3072]{2,1,0:T(8,128)(2,1)} %param.11) | data formatting | bytes 4718592 | tf_op args[0]
  116.6 38.0 %all-to-all-done = bf16[4,96,3072]{1,0,2:T(4,128)(2,1)} async-done(((bf16[4,96,3072]{1,0,2:T(4,128)(2,1)}), bf16[4,96,3072]{1,0,2:T(4,128)(2,1)}, u32[]{:S(2)}, u32[]{:S(2)}) %all-to-all-start) | async-done | bytes 2359328 | tf_op jit(solution)/shard_map/all_to_all | solution.py:61
  154.6 5.8 %copy.48 = bf16[4,4,96,768]{3,2,1,0:T(8,128)(2,1)} copy(bf16[4,4,96,768]{2,0,3,1:T(4,128)(2,1)} %bitcast.12) | data formatting | bytes 4718592 | tf_op jit(solution)/shard_map/all_to_all | solution.py:61
  160.4 11.9 %pad_maximum_fusion = bf16[2,12,384,768]{3,2,1,0:T(8,128)(2,1)} fusion(bf16[2,4,384,768]{3,2,1,0:T(8,128)(2,1)} %collective-permute-done.1, bf16[1,4,384,768]{3,2,1,0:T(8,128)(2,1)} %bitcast.71, bf16[1,4,384,768]{3,2,1,0:T(8,128)(2,1)S(1)} %bitcast.69, bf16[2,4,384,768]{3,2,1,0:T(8,128)(2,1)} %collective-permute-done), kind=kLoop, calls=%fused_computation.22 | loop fusion | flops 21233664 | bytes 28311552 | tf_op jit(solution)/shard_map/concatenate | solution.py:20
  172.3 18.7 %copy.56 = bf16[2,12,384,768]{2,3,1,0:T(8,128)(2,1)} copy(bf16[2,12,384,768]{3,2,1,0:T(8,128)(2,1)} %pad_maximum_fusion) | data formatting | bytes 28311552 | tf_op jit(solution)/shard_map/while | solution.py:89
  191.0 202.3 %while.42 = (s32[]{:T(128)}, bf16[4,384,768]{1,2,0:T(8,128)(2,1)}, s32[4]{0:T(128)S(1)}, s32[4,8]{1,0:T(4,128)}, s32[4]{0:T(128)S(1)}, /*index=5*/bf16[4,384,768...) while((s32[]{:T(128)}, bf16[4,384,768]{1,2,0:T(8,128)(2,1)}, ...), condition=%wide.region_7.8_spmd, body=%wide.region_0.7_spmd.sunk | while | flops 461546496 | bytes 27289812 | solution.py:89
  196.4 43.8 %while.43 = (s32[]{:T(128)}, f32[384,6]{0,1:T(8,128)S(1)}, f32[384,6]{0,1:T(8,128)S(1)}, f32[384,6,128]{2,0,1:T(8,128)S(1)}, s32[]{:T(128)}, /*index=5*/s32[8]{0...) while((s32[]{:T(128)}, f32[384,6]{0,1:T(8,128)S(1)}, ...), condition=%wide.region_6.6_spmd, body=%wide.region_1.5_spmd.sunk | while | flops 460956672 | bytes 17234280 | solution.py:87
  196.9 5.6 %conditional.2 = ((f32[384,6]{0,1:T(8,128)S(1)}, f32[384,6]{0,1:T(8,128)S(1)}, f32[384,6,128]{2,0,1:T(8,128)S(1)})) conditional(s32[]{:T(128)} %convert_element_type.45, (f32[384,6]{0,1:T(8,128)S(1)}, f32[384,6]{0,1:T(8,128)S(1)}, f32[384,6,128]{2,0,1:T(8,128)S(1)}) %tuple.102, (s32[]{:T(128)}, s32[8]{0:T(128)S(1)}, s32[]{:T(128)}, ...), branch_computations={%region_2.1_spmd, %region_3.4_spmd} | conditional | flops 460956672 | bytes 17234076 | solution.py:49
  203.1 5.6 %conditional.2 = ((f32[384,6]{0,1:T(8,128)S(1)}, f32[384,6]{0,1:T(8,128)S(1)}, f32[384,6,128]{2,0,1:T(8,128)S(1)})) conditional(s32[]{:T(128)} %convert_element_type.45, (f32[384,6]{0,1:T(8,128)S(1)}, f32[384,6]{0,1:T(8,128)S(1)}, f32[384,6,128]{2,0,1:T(8,128)S(1)}) %tuple.102, (s32[]{:T(128)}, s32[8]{0:T(128)S(1)}, s32[]{:T(128)}, ...), branch_computations={%region_2.1_spmd, %region_3.4_spmd} | conditional | flops 460956672 | bytes 17234076 | solution.py:49
  221.6 5.6 %conditional.2 = ((f32[384,6]{0,1:T(8,128)S(1)}, f32[384,6]{0,1:T(8,128)S(1)}, f32[384,6,128]{2,0,1:T(8,128)S(1)})) conditional(s32[]{:T(128)} %convert_element_type.45, (f32[384,6]{0,1:T(8,128)S(1)}, f32[384,6]{0,1:T(8,128)S(1)}, f32[384,6,128]{2,0,1:T(8,128)S(1)}) %tuple.102, (s32[]{:T(128)}, s32[8]{0:T(128)S(1)}, s32[]{:T(128)}, ...), branch_computations={%region_2.1_spmd, %region_3.4_spmd} | conditional | flops 460956672 | bytes 17234076 | solution.py:49
  234.0 5.6 %conditional.2 = ((f32[384,6]{0,1:T(8,128)S(1)}, f32[384,6]{0,1:T(8,128)S(1)}, f32[384,6,128]{2,0,1:T(8,128)S(1)})) conditional(s32[]{:T(128)} %convert_element_type.45, (f32[384,6]{0,1:T(8,128)S(1)}, f32[384,6]{0,1:T(8,128)S(1)}, f32[384,6,128]{2,0,1:T(8,128)S(1)}) %tuple.102, (s32[]{:T(128)}, s32[8]{0:T(128)S(1)}, s32[]{:T(128)}, ...), branch_computations={%region_2.1_spmd, %region_3.4_spmd} | conditional | flops 460956672 | bytes 17234076 | solution.py:49
  246.9 43.8 %while.43 = (s32[]{:T(128)}, f32[384,6]{0,1:T(8,128)S(1)}, f32[384,6]{0,1:T(8,128)S(1)}, f32[384,6,128]{2,0,1:T(8,128)S(1)}, s32[]{:T(128)}, /*index=5*/s32[8]{0...) while((s32[]{:T(128)}, f32[384,6]{0,1:T(8,128)S(1)}, ...), condition=%wide.region_6.6_spmd, body=%wide.region_1.5_spmd.sunk | while | flops 460956672 | bytes 17234280 | solution.py:87
  278.4 5.6 %conditional.2 = ((f32[384,6]{0,1:T(8,128)S(1)}, f32[384,6]{0,1:T(8,128)S(1)}, f32[384,6,128]{2,0,1:T(8,128)S(1)})) conditional(s32[]{:T(128)} %convert_element_type.45, (f32[384,6]{0,1:T(8,128)S(1)}, f32[384,6]{0,1:T(8,128)S(1)}, f32[384,6,128]{2,0,1:T(8,128)S(1)}) %tuple.102, (s32[]{:T(128)}, s32[8]{0:T(128)S(1)}, s32[]{:T(128)}, ...), branch_computations={%region_2.1_spmd, %region_3.4_spmd} | conditional | flops 460956672 | bytes 17234076 | solution.py:49
  297.5 43.8 %while.43 = (s32[]{:T(128)}, f32[384,6]{0,1:T(8,128)S(1)}, f32[384,6]{0,1:T(8,128)S(1)}, f32[384,6,128]{2,0,1:T(8,128)S(1)}, s32[]{:T(128)}, /*index=5*/s32[8]{0...) while((s32[]{:T(128)}, f32[384,6]{0,1:T(8,128)S(1)}, ...), condition=%wide.region_6.6_spmd, body=%wide.region_1.5_spmd.sunk | while | flops 460956672 | bytes 17234280 | solution.py:87
  298.1 5.6 %conditional.2 = ((f32[384,6]{0,1:T(8,128)S(1)}, f32[384,6]{0,1:T(8,128)S(1)}, f32[384,6,128]{2,0,1:T(8,128)S(1)})) conditional(s32[]{:T(128)} %convert_element_type.45, (f32[384,6]{0,1:T(8,128)S(1)}, f32[384,6]{0,1:T(8,128)S(1)}, f32[384,6,128]{2,0,1:T(8,128)S(1)}) %tuple.102, (s32[]{:T(128)}, s32[8]{0:T(128)S(1)}, s32[]{:T(128)}, ...), branch_computations={%region_2.1_spmd, %region_3.4_spmd} | conditional | flops 460956672 | bytes 17234076 | solution.py:49
  316.6 5.6 %conditional.2 = ((f32[384,6]{0,1:T(8,128)S(1)}, f32[384,6]{0,1:T(8,128)S(1)}, f32[384,6,128]{2,0,1:T(8,128)S(1)})) conditional(s32[]{:T(128)} %convert_element_type.45, (f32[384,6]{0,1:T(8,128)S(1)}, f32[384,6]{0,1:T(8,128)S(1)}, f32[384,6,128]{2,0,1:T(8,128)S(1)}) %tuple.102, (s32[]{:T(128)}, s32[8]{0:T(128)S(1)}, s32[]{:T(128)}, ...), branch_computations={%region_2.1_spmd, %region_3.4_spmd} | conditional | flops 460956672 | bytes 17234076 | solution.py:49
  329.0 5.6 %conditional.2 = ((f32[384,6]{0,1:T(8,128)S(1)}, f32[384,6]{0,1:T(8,128)S(1)}, f32[384,6,128]{2,0,1:T(8,128)S(1)})) conditional(s32[]{:T(128)} %convert_element_type.45, (f32[384,6]{0,1:T(8,128)S(1)}, f32[384,6]{0,1:T(8,128)S(1)}, f32[384,6,128]{2,0,1:T(8,128)S(1)}) %tuple.102, (s32[]{:T(128)}, s32[8]{0:T(128)S(1)}, s32[]{:T(128)}, ...), branch_computations={%region_2.1_spmd, %region_3.4_spmd} | conditional | flops 460956672 | bytes 17234076 | solution.py:49
  348.1 43.8 %while.43 = (s32[]{:T(128)}, f32[384,6]{0,1:T(8,128)S(1)}, f32[384,6]{0,1:T(8,128)S(1)}, f32[384,6,128]{2,0,1:T(8,128)S(1)}, s32[]{:T(128)}, /*index=5*/s32[8]{0...) while((s32[]{:T(128)}, f32[384,6]{0,1:T(8,128)S(1)}, ...), condition=%wide.region_6.6_spmd, body=%wide.region_1.5_spmd.sunk | while | flops 460956672 | bytes 17234280 | solution.py:87
  397.4 20.4 %all_to_all.66 = bf16[4,384,768]{2,0,1:T(4,128)(2,1)S(1)} all-to-all(bf16[4,384,768]{2,0,1:T(4,128)(2,1)S(1)} %copy.57), channel_id=1, replica_groups=mesh['head'=4,'ctx'=64] {'head'}, dimensions={1} | all-to-all | bytes 4718592 | tf_op jit(solution)/shard_map/all_to_all | solution.py:90
  (258 shorter events, 305.1 us)
Async XLA Ops:
  5.7 41.9 %all-to-all-start.1 = ((bf16[4,96,3072]{1,0,2:T(4,128)(2,1)}), bf16[4,96,3072]{1,0,2:T(4,128)(2,1)S(1)}, u32[]{:S(2)}, u32[]{:S(2)}) async-start(bf16[4,96,3072]{1,0,2:T(4,128)(2,1)} %copy.49), calls=%async_computation.1 | async-start | bytes 6291456 | tf_op jit(solution)/shard_map/all_to_all | solution.py:62
  47.5 1.7 copy-start
  49.3 41.4 %all-to-all-start.2 = ((bf16[4,96,3072]{1,0,2:T(4,128)(2,1)}), bf16[4,96,3072]{1,0,2:T(4,128)(2,1)}, u32[]{:S(2)}, u32[]{:S(2)}) async-start(bf16[4,96,3072]{1,0,2:T(4,128)(2,1)} %copy.52), calls=%async_computation.2 | async-start | bytes 6291456 | tf_op jit(solution)/shard_map/all_to_all | solution.py:63
  100.6 59.8 %collective-permute-start = (bf16[2,4,384,768]{3,2,1,0:T(8,128)(2,1)}, bf16[2,4,384,768]{3,2,1,0:T(8,128)(2,1)}, u32[]{:S(2)}, u32[]{:S(2)}) collective-permute-start(bf16[2,4,384,768]{3,2,1,0:T(8,128)(2,1)} %pad_maximum_fusion.1), channel_id=1, source_target_pairs={{0,1},{1,2},{2,3},{3,4},{4,5},{5,6},{6,7},{7,8},{8,9},{9,10},{10,1... | collective-permute-start | bytes 14155784 | tf_op jit(solution)/shard_map/ppermute | solution.py:16
  102.5 57.9 %collective-permute-start.1 = (bf16[2,4,384,768]{3,2,1,0:T(8,128)(2,1)}, bf16[2,4,384,768]{3,2,1,0:T(8,128)(2,1)}, u32[]{:S(2)}, u32[]{:S(2)}) collective-permute-start(bf16[2,4,384,768]{3,2,1,0:T(8,128)(2,1)} %pad_maximum_fusion.1), channel_id=1, source_target_pairs={{1,0},{2,1},{3,2},{4,3},{5,4},{6,5},{7,6},{8,7},{9,8},{10,9},{11,1... | collective-permute-start | bytes 14155784 | tf_op jit(solution)/shard_map/ppermute | solution.py:19
  111.9 42.7 %all-to-all-start = ((bf16[4,96,3072]{1,0,2:T(4,128)(2,1)}), bf16[4,96,3072]{1,0,2:T(4,128)(2,1)}, u32[]{:S(2)}, u32[]{:S(2)}) async-start(bf16[4,96,3072]{1,0,2:T(4,128)(2,1)} %copy.46), calls=%async_computation | async-start | bytes 6291456 | tf_op jit(solution)/shard_map/all_to_all | solution.py:61
  172.3 18.7 %copy-start.1 = (s32[4]{0:T(128)S(1)}, s32[4]{0:T(128)}, u32[]{:S(2)}) copy-start(s32[4]{0:T(128)} %param.15) | copy-start | bytes 52
where the time goes:
time: 423 us; the launch traced here: 420 us
  local copies, waits for them, and re-layouts  135 us (32%)
  waiting for transfers between devices  102 us (24%)
  matrix products  65 us (15%)
  loops' own time  44.7 us (11%)
  other arithmetic  33.6 us (8%)
  blocking collectives  20.4 us (5%)
  starting transfers between devices  19.2 us (5%)
    dot_general x28, matrix products, update(): jnp.einsum('qhk,khd->qhd', weights, values_tile, preferred_element_type=j...  45.7 us
    slice x28, local copies, waits for them, and re-layouts, update(): values_tile = kv_tile[1].reshape(kv_tile.shape[1], -1, DH)  38.3 us
    all_to_all x1, waiting for transfers between devices, body(): lax.all_to_all(query, 'head', split_axis=2, concat_axis=1, tiled=True)  38 us
    all_to_all x1, waiting for transfers between devices, body(): lax.all_to_all(values_in, 'head', split_axis=2, concat_axis=1, tiled=True)  32.4 us
    all_to_all x1, waiting for transfers between devices, body(): lax.all_to_all(keys_in, 'head', split_axis=2, concat_axis=1, tiled=True)  31.9 us
    while x2, local copies, waits for them, and re-layouts, body(): outputs = lax.map(per_tile, jnp.arange(tiles_dev))  22.8 us
    all_to_all x1, blocking collectives, body(): lax.all_to_all(outputs, 'head', split_axis=1, concat_axis=2, tiled=True)  20.4 us
    dot_general x28, matrix products, update(): jnp.einsum('qhd,khd->qhk', query_tile, keys_tile, preferred_element_type=...  19.3 us
  transfers between devices with their start and end apart: 5, of which 3 were waited for; matrix products, arithmetic and copies ran while one was open for 5% of the time, Pallas kernels for 0%

commit v1 on v0

v1 whole, which is shorter than its diff:
```python
import jax
import jax.numpy as jnp
from jax import lax
from jax.experimental import pallas as pl
from jax.experimental.pallas import tpu as pltpu
from jax.sharding import PartitionSpec as P

DH = 128
GROUP = 4
EXP2_SCALE = DH ** -0.5 * 1.4426950408889634
MASKED = 1e30
MESH = pl.DeviceIdType.MESH


def build_kernel(n_head, n_ctx, tiles, rows, heads, most):
    tok = n_head * rows

    def kernel(slots_ref, count_ref, q_ref, k_ref, v_ref, out_ref, *scratch):
        kwin, vwin = scratch[:heads], scratch[heads:2 * heads]
        q_all, v_all, o_all, rx, tx, win, wtx, o_rx, o_tx = scratch[2 * heads:]
        me_h, me_c = lax.axis_index("head"), lax.axis_index("ctx")
        first_slot = (me_c - 1) * tiles
        up, down = lax.rem(me_c + 1, n_ctx), lax.rem(me_c + n_ctx - 1, n_ctx)
        others = [lax.rem(me_h + step, n_head) for step in (1, n_head - 1, *range(2, n_head - 1))]

        barrier = pltpu.get_barrier_semaphore()
        for other in others:
            pl.semaphore_signal(barrier, inc=1, device_id={"head": other}, device_id_type=MESH)
        for other in (up, down):
            pl.semaphore_signal(barrier, inc=1, device_id={"ctx": other}, device_id_type=MESH)
        pl.semaphore_wait(barrier, len(others) + 2)

        def head_columns(owner, g):
            return pl.ds(pl.multiple_of((owner * heads + g) * DH, DH), DH)

        def token_rows(owner):
            return pl.ds(pl.multiple_of(owner * rows, rows), rows)

        def landing(which, g):
            if which == 0:
                return kwin[g].at[tiles:2 * tiles]
            return (v_all if which == 1 else q_all).at[g]

        def send_inputs(g):
            for which, source in enumerate((k_ref, v_ref, q_ref)):
                target = landing(which, g).at[:, token_rows(me_h), :]
                for other in others:
                    pltpu.make_async_remote_copy(
                        src_ref=source.at[:, :, head_columns(other, g)],
                        dst_ref=target,
                        send_sem=tx.at[which],
                        recv_sem=rx.at[which, g],
                        device_id={"head": other},
                        device_id_type=MESH,
                    ).start()
                pltpu.make_async_copy(
                    source.at[:, :, head_columns(me_h, g)], target, rx.at[which, g]
                ).start()

        def await_bytes(ref, sem):
            pltpu.make_async_copy(ref, ref, sem).wait()

        def send_window(which, window, g):
            for other, place in ((up, 0), (down, 2 * tiles)):
                pltpu.make_async_remote_copy(
                    src_ref=window[g].at[tiles:2 * tiles],
                    dst_ref=window[g].at[place:place + tiles],
                    send_sem=wtx.at[which, g],
                    recv_sem=win.at[which, g],
                    device_id={"ctx": other},
                    device_id_type=MESH,
                ).start()

        def share(g):
            await_bytes(landing(0, g), rx.at[0, g])
            send_window(0, kwin, g)
            await_bytes(landing(1, g), rx.at[1, g])

            def turn(t, carry):
                vwin[g][tiles + t] = v_all[g, t].T
                return carry

            lax.fori_loop(0, tiles, turn, 0)
            send_window(1, vwin, g)

        def compute(g):
            def one_tile(t, carry):
                query_t = q_all[g, t].T
                live = count_ref[t]
                top = jnp.full((1, tok), -MASKED, jnp.float32)
                total = jnp.zeros((1, tok), jnp.float32)
                out_t = jnp.zeros((DH, tok), jnp.float32)
                for base in range(0, most, GROUP):
                    scores, values, shifts = [], [], []
                    new_top = top
                    for p in range(base, base + GROUP):
                        slot = jnp.clip(slots_ref[t, p] - first_slot, 0, 3 * tiles - 1)
                        s = jnp.dot(kwin[g][slot], query_t, preferred_element_type=jnp.float32)
                        shift = jnp.where(p < live, 0.0, MASKED).astype(jnp.float32)
                        new_top = jnp.maximum(new_top, jnp.max(s, axis=0, keepdims=True) - shift)
                        scores.append(s)
                        values.append(vwin[g][slot])
                        shifts.append(shift)
                    top_scaled = new_top * EXP2_SCALE
                    old_factor = jnp.exp2(top * EXP2_SCALE - top_scaled)
                    total = total * old_factor
                    out_t = out_t * old_factor
                    for i in range(0, GROUP, 2):
                        weights = []
                        for s, shift in zip(scores[i:i + 2], shifts[i:i + 2]):
                            expo = jnp.exp2(s * EXP2_SCALE - (top_scaled + shift))
                            total = total + jnp.sum(expo, axis=0, keepdims=True)
                            weights.append(expo.astype(jnp.bfloat16))
                        out_t = out_t + jnp.dot(
                            jnp.concatenate(values[i:i + 2], axis=1),
                            jnp.concatenate(weights, axis=0),
                            preferred_element_type=jnp.float32,
                        )
                    top = new_top
                o_all[g, t] = (out_t / total).T.astype(jnp.bfloat16)
                return carry

            lax.fori_loop(0, tiles, one_tile, 0)

        def send_outputs(g):
            target = out_ref.at[:, :, head_columns(me_h, g)]
            for other in others:
                pltpu.make_async_remote_copy(
                    src_ref=o_all.at[g, :, token_rows(other), :],
                    dst_ref=target,
                    send_sem=o_tx.at[g],
                    recv_sem=o_rx.at[g],
                    device_id={"head": other},
                    device_id_type=MESH,
                ).start()
            pltpu.make_async_copy(
                o_all.at[g, :, token_rows(me_h), :], target, o_rx.at[g]
            ).start()

        send_inputs(0)
        if heads > 1:
            send_inputs(1)
        share(0)
        for g in range(heads):
            if g + 2 < heads:
                send_inputs(g + 2)
            if g + 1 < heads:
                share(g + 1)
            await_bytes(q_all.at[g], rx.at[2, g])
            await_bytes(kwin[g].at[:2 * tiles], win.at[0, g])
            await_bytes(vwin[g].at[:2 * tiles], win.at[1, g])
            compute(g)
            send_outputs(g)

        sent = tiles * (n_head - 1) // n_head
        for which, source in enumerate((k_ref, v_ref, q_ref)):
            await_bytes(source.at[:sent], tx.at[which])
        for g in range(heads):
            await_bytes(kwin[g].at[:2 * tiles], wtx.at[0, g])
            await_bytes(vwin[g].at[:2 * tiles], wtx.at[1, g])
            await_bytes(o_all.at[g, :, :(n_head - 1) * rows, :], o_tx.at[g])
            await_bytes(o_all.at[g], o_rx.at[g])

    return kernel


def solution(mesh):
    n_head, n_ctx = mesh.shape["head"], mesh.shape["ctx"]

    def body(query, keys_in, values_in, pair_keys, pair_count):
        tiles, rows, width = query.shape
        most = pair_keys.shape[1]
        tok, heads = rows * n_head, width // DH // n_head
        units = tiles * most * heads
        dma = pltpu.SemaphoreType.DMA
        scratch = [pltpu.VMEM((3 * tiles, tok, DH), jnp.bfloat16)] * heads
        scratch += [pltpu.VMEM((3 * tiles, DH, tok), jnp.bfloat16)] * heads
        scratch += [pltpu.VMEM((heads, tiles, tok, DH), jnp.bfloat16)] * 3
        scratch += [dma((3, heads)), dma((3,)), dma((2, heads)), dma((2, heads)), dma((heads,)), dma((heads,))]
        smem = pl.BlockSpec(memory_space=pltpu.SMEM)
        anywhere = pl.BlockSpec(memory_space=pl.ANY)
        return pl.pallas_call(
            build_kernel(n_head, n_ctx, tiles, rows, heads, most),
            out_shape=jax.ShapeDtypeStruct(query.shape, query.dtype),
            in_specs=[smem, smem, anywhere, anywhere, anywhere],
            out_specs=anywhere,
            scratch_shapes=scratch,
            compiler_params=pltpu.CompilerParams(
                collective_id=0, has_side_effects=True, vmem_limit_bytes=56 * 2 ** 20
            ),
            cost_estimate=pl.CostEstimate(
                flops=units * 4 * tok * tok * DH,
                bytes_accessed=8 * query.size,
                transcendentals=units * tok * tok,
            ),
        )(pair_keys, pair_count, query, keys_in, values_in)

    tokens = P("ctx", "head", None)
    return jax.shard_map(
        body,
        mesh=mesh,
        in_specs=(tokens, tokens, tokens, P("ctx", None), P("ctx")),
        out_specs=tokens,
        check_vma=False,
    )
```

time: 423 us -> 122 us (0.29)
  the two profiles are of different devices: /device:TPU:88 before, /device:TPU:122 now
where the time goes in v1:
time: 122 us; the launch traced here: 120 us
  Pallas kernels  116 us (95%)
  local copies, waits for them, and re-layouts  3.22 us (3%)
    pallas_call x1, Pallas kernels, body(): pl.pallas_call(build_kernel(n_head, n_ctx, tiles, rows, heads, most), out...  116 us
    unnamed x1, local copies, waits for them, and re-layouts  3.22 us

profile of v1, /device:TPU:122, one launch (start us, length us, event | category | flops | bytes accessed | tf_op | source)
XLA Modules:
  0.0 119.6 jit_solution(12618181357650287276)
XLA Ops:
  0.0 116.4 %shard_map.55 = bf16[4,96,3072]{2,1,0:T(8,128)(2,1)} custom-call(s32[4,8]{1,0:T(4,128)} %slots_ref.1, s32[4]{0:T(128)} %count_ref.1, bf16[4,96,3072]{2,1,0:T(8,128)(2,1)} %q_ref.1, bf16[4,96,3072]{2,1,0:T(8,128)(2,1)} %k_ref.1, bf16[4,96,3072]{2,1,0:T(8,128)(2,1)} %v_ref.1), custom_call_target="tpu_custom_call" | custom-call | flops 14495514624 | bytes 9437184 | tf_op jit(solution)/shard_map/pallas_call | solution.py:182
  116.4 3.2 %copy.7 = bf16[4,96,3072]{2,1,0:T(8,128)(2,1)} copy(bf16[4,96,3072]{2,1,0:T(8,128)(2,1)} %shard_map.55) | data formatting | bytes 4718592

commit v2 on v1

--- a/solution.py
+++ b/solution.py
@@ -1,3 +1,5 @@
+import functools
+
 import jax
 import jax.numpy as jnp
 from jax import lax
@@ -20,13 +22,12 @@
         q_all, v_all, o_all, rx, tx, win, wtx, o_rx, o_tx = scratch[2 * heads:]
         me_h, me_c = lax.axis_index("head"), lax.axis_index("ctx")
         first_slot = (me_c - 1) * tiles
-        up, down = lax.rem(me_c + 1, n_ctx), lax.rem(me_c + n_ctx - 1, n_ctx)
         others = [lax.rem(me_h + step, n_head) for step in (1, n_head - 1, *range(2, n_head - 1))]
 
         barrier = pltpu.get_barrier_semaphore()
         for other in others:
             pl.semaphore_signal(barrier, inc=1, device_id={"head": other}, device_id_type=MESH)
-        for other in (up, down):
+        for other in (lax.rem(me_c + 1, n_ctx), lax.rem(me_c + n_ctx - 1, n_ctx)):
             pl.semaphore_signal(barrier, inc=1, device_id={"ctx": other}, device_id_type=MESH)
         pl.semaphore_wait(barrier, len(others) + 2)
 
@@ -60,28 +61,44 @@
         def await_bytes(ref, sem):
             pltpu.make_async_copy(ref, ref, sem).wait()
 
-        def send_window(which, window, g):
-            for other, place in ((up, 0), (down, 2 * tiles)):
-                pltpu.make_async_remote_copy(
-                    src_ref=window[g].at[tiles:2 * tiles],
-                    dst_ref=window[g].at[place:place + tiles],
-                    send_sem=wtx.at[which, g],
-                    recv_sem=win.at[which, g],
-                    device_id={"ctx": other},
-                    device_id_type=MESH,
-                ).start()
-
-        def share(g):
+        def send_window(which, window, g, t):
+            own = window[g].at[tiles + t]
+            for side, (other, inside) in enumerate(((me_c + 1, me_c < n_ctx - 1), (me_c - 1, me_c > 0))):
+                @pl.when(inside)
+                def _():
+                    pltpu.make_async_remote_copy(
+                        src_ref=own,
+                        dst_ref=window[g].at[2 * tiles * side + t],
+                        send_sem=wtx.at[which, side, g],
+                        recv_sem=win.at[which, g],
+                        device_id={"ctx": other},
+                        device_id_type=MESH,
+                    ).start()
+
+                @pl.when(jnp.logical_not(inside))
+                def _():
+                    pltpu.make_async_copy(
+                        own, window[g].at[2 * tiles * (1 - side) + t], win.at[which, g]
+                    ).start()
+
+        def share_keys(g):
             await_bytes(landing(0, g), rx.at[0, g])
-            send_window(0, kwin, g)
+
+            def pass_on(t, carry):
+                send_window(0, kwin, g, t)
+                return carry
+
+            lax.fori_loop(0, tiles, pass_on, 0)
+
+        def share_values(g):
             await_bytes(landing(1, g), rx.at[1, g])
 
-            def turn(t, carry):
+            def pass_on(t, carry):
                 vwin[g][tiles + t] = v_all[g, t].T
+                send_window(1, vwin, g, t)
                 return carry
 
-            lax.fori_loop(0, tiles, turn, 0)
-            send_window(1, vwin, g)
+            lax.fori_loop(0, tiles, pass_on, 0)
 
         def compute(g):
             def one_tile(t, carry):
@@ -118,15 +135,19 @@
                         )
                     top = new_top
                 o_all[g, t] = (out_t / total).T.astype(jnp.bfloat16)
+                send_output(g, t)
+                for at, duty, ahead in ((0, share_keys, 1), (0, send_inputs, 3), (1, share_values, 1)):
+                    if g + ahead < heads:
+                        pl.when(t == at)(functools.partial(duty, g + ahead))
                 return carry
 
             lax.fori_loop(0, tiles, one_tile, 0)
 
-        def send_outputs(g):
-            target = out_ref.at[:, :, head_columns(me_h, g)]
+        def send_output(g, t):
+            target = out_ref.at[t, :, head_columns(me_h, g)]
             for other in others:
                 pltpu.make_async_remote_copy(
-                    src_ref=o_all.at[g, :, token_rows(other), :],
+                    src_ref=o_all.at[g, t, token_rows(other), :],
                     dst_ref=target,
                     send_sem=o_tx.at[g],
                     recv_sem=o_rx.at[g],
@@ -134,30 +155,30 @@
                     device_id_type=MESH,
                 ).start()
             pltpu.make_async_copy(
-                o_all.at[g, :, token_rows(me_h), :], target, o_rx.at[g]
+                o_all.at[g, t, token_rows(me_h), :], target, o_rx.at[g]
             ).start()
 
-        send_inputs(0)
-        if heads > 1:
-            send_inputs(1)
-        share(0)
+        for g in range(min(2, heads)):
+            send_inputs(g)
+        share_keys(0)
+        share_values(0)
+        if heads > 2:
+            send_inputs(2)
         for g in range(heads):
-            if g + 2 < heads:
-                send_inputs(g + 2)
-            if g + 1 < heads:
-                share(g + 1)
             await_bytes(q_all.at[g], rx.at[2, g])
             await_bytes(kwin[g].at[:2 * tiles], win.at[0, g])
             await_bytes(vwin[g].at[:2 * tiles], win.at[1, g])
             compute(g)
-            send_outputs(g)
 
         sent = tiles * (n_head - 1) // n_head
         for which, source in enumerate((k_ref, v_ref, q_ref)):
             await_bytes(source.at[:sent], tx.at[which])
         for g in range(heads):
-            await_bytes(kwin[g].at[:2 * tiles], wtx.at[0, g])
-            await_bytes(vwin[g].at[:2 * tiles], wtx.at[1, g])
+            for which, window in enumerate((kwin, vwin)):
+                for side, inside in enumerate((me_c < n_ctx - 1, me_c > 0)):
+                    pl.when(inside)(
+                        functools.partial(await_bytes, window[g].at[:tiles], wtx.at[which, side, g])
+                    )
             await_bytes(o_all.at[g, :, :(n_head - 1) * rows, :], o_tx.at[g])
             await_bytes(o_all.at[g], o_rx.at[g])
 
@@ -176,7 +197,7 @@
         scratch = [pltpu.VMEM((3 * tiles, tok, DH), jnp.bfloat16)] * heads
         scratch += [pltpu.VMEM((3 * tiles, DH, tok), jnp.bfloat16)] * heads
         scratch += [pltpu.VMEM((heads, tiles, tok, DH), jnp.bfloat16)] * 3
-        scratch += [dma((3, heads)), dma((3,)), dma((2, heads)), dma((2, heads)), dma((heads,)), dma((heads,))]
+        scratch += [dma((3, heads)), dma((3,)), dma((2, heads)), dma((2, 2, heads)), dma((heads,)), dma((heads,))]
         smem = pl.BlockSpec(memory_space=pltpu.SMEM)
         anywhere = pl.BlockSpec(memory_space=pl.ANY)
         return pl.pallas_call(

time: 122 us -> 116 us (0.951)
  the two profiles are of different devices: /device:TPU:122 before, /device:TPU:2 now
where the time goes in v2:
time: 116 us; the launch traced here: 115 us
  Pallas kernels  112 us (97%)
  local copies, waits for them, and re-layouts  3.22 us (3%)
    pallas_call x1, Pallas kernels, body(): pl.pallas_call(build_kernel(n_head, n_ctx, tiles, rows, heads, most), out...  112 us
    unnamed x1, local copies, waits for them, and re-layouts  3.22 us

profile of v2, /device:TPU:2, one launch (start us, length us, event | category | flops | bytes accessed | tf_op | source)
XLA Modules:
  0.0 115.5 jit_solution(2173301721424806020)
XLA Ops:
  0.0 112.3 %shard_map.55 = bf16[4,96,3072]{2,1,0:T(8,128)(2,1)} custom-call(s32[4,8]{1,0:T(4,128)} %slots_ref.1, s32[4]{0:T(128)} %count_ref.1, bf16[4,96,3072]{2,1,0:T(8,128)(2,1)} %q_ref.1, bf16[4,96,3072]{2,1,0:T(8,128)(2,1)} %k_ref.1, bf16[4,96,3072]{2,1,0:T(8,128)(2,1)} %v_ref.1), custom_call_target="tpu_custom_call" | custom-call | flops 14495514624 | bytes 9437184 | tf_op jit(solution)/shard_map/pallas_call | solution.py:203
  112.3 3.2 %copy.7 = bf16[4,96,3072]{2,1,0:T(8,128)(2,1)} copy(bf16[4,96,3072]{2,1,0:T(8,128)(2,1)} %shard_map.55) | data formatting | bytes 4718592

commit v3 on v2

v3 whole, which is shorter than its diff:
```python
import functools

import jax
import jax.numpy as jnp
from jax import lax
from jax.experimental import pallas as pl
from jax.experimental.pallas import tpu as pltpu
from jax.sharding import PartitionSpec as P

DH = 128
EXP2_SCALE = DH ** -0.5 * 1.4426950408889634
MASKED = 1e30
MESH = pl.DeviceIdType.MESH


def build_kernel(n_head, n_ctx, tiles, rows, heads, most):
    tok = n_head * rows

    def kernel(slots_ref, count_ref, q_ref, k_ref, v_ref, out_ref, *scratch):
        kwin, vwin = scratch[:heads], scratch[heads:2 * heads]
        q_all, k_all, o_all, rx, tx, win, wtx, o_rx, o_tx = scratch[2 * heads:]
        me_h, me_c = lax.axis_index("head"), lax.axis_index("ctx")
        first_slot = (me_c - 1) * tiles
        others = [lax.rem(me_h + step, n_head) for step in (1, n_head - 1, *range(2, n_head - 1))]

        barrier = pltpu.get_barrier_semaphore()
        for other in others:
            pl.semaphore_signal(barrier, inc=1, device_id={"head": other}, device_id_type=MESH)
        ctx_sides = ((me_c + 1, me_c < n_ctx - 1), (me_c - 1, me_c > 0))
        for other, inside in ctx_sides:
            @pl.when(inside)
            def _():
                pl.semaphore_signal(barrier, inc=1, device_id={"ctx": other}, device_id_type=MESH)
        at_edge = jnp.logical_or(me_c == 0, me_c == n_ctx - 1)
        for edge, partners in ((at_edge, len(others) + 1), (jnp.logical_not(at_edge), len(others) + 2)):
            pl.when(edge)(functools.partial(pl.semaphore_wait, barrier, partners))

        def head_columns(owner, g):
            return pl.ds(pl.multiple_of((owner * heads + g) * DH, DH), DH)

        def token_rows(owner):
            return pl.ds(pl.multiple_of(owner * rows, rows), rows)

        def landing(which, g):
            if which == 1:
                return vwin[g].at[tiles:2 * tiles]
            return (k_all if which == 0 else q_all).at[g]

        def send_inputs(kinds, g):
            for which in kinds:
                source = (k_ref, v_ref, q_ref)[which]
                target = landing(which, g).at[:, token_rows(me_h), :]
                for other in others:
                    pltpu.make_async_remote_copy(
                        src_ref=source.at[:, :, head_columns(other, g)],
                        dst_ref=target,
                        send_sem=tx.at[which],
                        recv_sem=rx.at[which, g],
                        device_id={"head": other},
                        device_id_type=MESH,
                    ).start()
                pltpu.make_async_copy(
                    source.at[:, :, head_columns(me_h, g)], target, rx.at[which, g]
                ).start()

        def await_bytes(ref, sem):
            pltpu.make_async_copy(ref, ref, sem).wait()

        def send_window(which, window, g, t):
            own = window[g].at[tiles + t]
            for side, (other, inside) in enumerate(ctx_sides):
                @pl.when(inside)
                def _():
                    pltpu.make_async_remote_copy(
                        src_ref=own,
                        dst_ref=window[g].at[2 * tiles * side + t],
                        send_sem=wtx.at[which, side, g],
                        recv_sem=win.at[which, g],
                        device_id={"ctx": other},
                        device_id_type=MESH,
                    ).start()

                @pl.when(jnp.logical_not(inside))
                def _():
                    pltpu.make_async_copy(
                        own, window[g].at[2 * tiles * (1 - side) + t], win.at[which, g]
                    ).start()

        def share_keys(g):
            await_bytes(landing(0, g), rx.at[0, g])

            def pass_on(t, carry):
                kwin[g][tiles + t] = k_all[g, t].T
                send_window(0, kwin, g, t)
                return carry

            lax.fori_loop(0, tiles, pass_on, 0)

        def share_values(g):
            await_bytes(landing(1, g), rx.at[1, g])

            def pass_on(t, carry):
                send_window(1, vwin, g, t)
                return carry

            lax.fori_loop(0, tiles, pass_on, 0)

        def compute(g, duties):
            def one_tile(t, carry):
                query = q_all[g, t]
                live = count_ref[t]
                shifts = [jnp.where(p < live, 0.0, MASKED).astype(jnp.float32) for p in range(most)]
                slots = [jnp.clip(slots_ref[t, p] - first_slot, 0, 3 * tiles - 1) for p in range(most)]
                scores, top = [], jnp.full((tok, DH), -MASKED, jnp.float32)
                for p in range(0, most, 2):
                    keys = jnp.concatenate([kwin[g][slots[p]], kwin[g][slots[p + 1]]], axis=1)
                    both = jnp.dot(query, keys, preferred_element_type=jnp.float32)
                    for s, shift in zip((both[:, :tok], both[:, tok:]), shifts[p:p + 2]):
                        most_of = s[:, :DH]
                        for at in range(DH, tok, DH):
                            most_of = jnp.maximum(most_of, s[:, at:at + DH])
                        top = jnp.maximum(top, most_of - shift)
                        scores.append(s)
                top = jnp.max(top, axis=1, keepdims=True) * EXP2_SCALE
                ones = jnp.ones((2 * tok, DH), jnp.bfloat16)
                merged = jnp.zeros((tok, 2 * DH), jnp.float32)
                for p in range(0, most, 2):
                    weights = [
                        jnp.exp2(s * EXP2_SCALE - (top + shift)).astype(jnp.bfloat16)
                        for s, shift in zip(scores[p:p + 2], shifts[p:p + 2])
                    ]
                    values = jnp.concatenate([vwin[g][slots[p]], vwin[g][slots[p + 1]]], axis=0)
                    merged = merged + jnp.dot(
                        jnp.concatenate(weights, axis=1),
                        jnp.concatenate([values, ones], axis=1),
                        preferred_element_type=jnp.float32,
                    )
                o_all[g, t] = (merged[:, :DH] / merged[:, DH:]).astype(jnp.bfloat16)
                if g == heads - 1:
                    send_output(g, t)
                for at, duty in duties:
                    pl.when(t == at)(duty)
                return carry

            lax.fori_loop(0, tiles, one_tile, 0)

        def send_output(g, t):
            target = out_ref.at[t, :, head_columns(me_h, g)]
            for other in others:
                pltpu.make_async_remote_copy(
                    src_ref=o_all.at[g, t, token_rows(other), :],
                    dst_ref=target,
                    send_sem=o_tx.at[g],
                    recv_sem=o_rx.at[g],
                    device_id={"head": other},
                    device_id_type=MESH,
                ).start()
            pltpu.make_async_copy(
                o_all.at[g, t, token_rows(me_h), :], target, o_rx.at[g]
            ).start()

        def send_outputs(g):
            def one_tile(t, carry):
                send_output(g, t)
                return carry

            lax.fori_loop(0, tiles, one_tile, 0)

        def later(duty, *args):
            return functools.partial(duty, *args) if args[-1] < heads else lambda: None

        send_inputs((0, 1, 2), 0)
        later(send_inputs, (0, 1), 1)()
        share_keys(0)
        share_values(0)
        later(send_inputs, (2,), 1)()
        later(send_inputs, (0, 1), 2)()
        for g in range(heads):
            duties = [(0, later(send_inputs, (0, 1), g + 3)), (0, later(send_inputs, (2,), g + 2))]
            sharing = [(0, later(share_keys, g + 1)), (1, later(share_values, g + 1))]
            if g < heads // 2:
                duties = sharing + duties
            else:
                for _, duty in sharing:
                    duty()
            if g == heads - 2:
                duties += [(min(held, tiles - 1), later(send_outputs, held)) for held in range(g)]
            elif g == heads - 1 and g > 0:
                duties.append((0, later(send_outputs, g - 1)))
            await_bytes(q_all.at[g], rx.at[2, g])
            await_bytes(kwin[g].at[:2 * tiles], win.at[0, g])
            await_bytes(vwin[g].at[:2 * tiles], win.at[1, g])
            compute(g, duties)

        sent = tiles * (n_head - 1) // n_head
        for which, source in enumerate((k_ref, v_ref, q_ref)):
            await_bytes(source.at[:sent], tx.at[which])
        for g in range(heads):
            for which, window in enumerate((kwin, vwin)):
                for side, (_, inside) in enumerate(ctx_sides):
                    pl.when(inside)(
                        functools.partial(await_bytes, window[g].at[:tiles], wtx.at[which, side, g])
                    )
            await_bytes(o_all.at[g, :, :(n_head - 1) * rows, :], o_tx.at[g])
            await_bytes(o_all.at[g], o_rx.at[g])

    return kernel


def solution(mesh):
    n_head, n_ctx = mesh.shape["head"], mesh.shape["ctx"]

    def body(query, keys_in, values_in, pair_keys, pair_count):
        tiles, rows, width = query.shape
        most = pair_keys.shape[1]
        tok, heads = rows * n_head, width // DH // n_head
        units = tiles * most * heads
        dma = pltpu.SemaphoreType.DMA
        scratch = [pltpu.VMEM((3 * tiles, DH, tok), jnp.bfloat16)] * heads
        scratch += [pltpu.VMEM((3 * tiles, tok, DH), jnp.bfloat16)] * heads
        scratch += [pltpu.VMEM((heads, tiles, tok, DH), jnp.bfloat16)] * 3
        scratch += [dma((3, heads)), dma((3,)), dma((2, heads)), dma((2, 2, heads)), dma((heads,)), dma((heads,))]
        smem = pl.BlockSpec(memory_space=pltpu.SMEM)
        anywhere = pl.BlockSpec(memory_space=pl.ANY)
        return pl.pallas_call(
            build_kernel(n_head, n_ctx, tiles, rows, heads, most),
            out_shape=jax.ShapeDtypeStruct(query.shape, query.dtype),
            in_specs=[smem, smem, anywhere, anywhere, anywhere],
            out_specs=anywhere,
            scratch_shapes=scratch,
            compiler_params=pltpu.CompilerParams(
                collective_id=0, has_side_effects=True, vmem_limit_bytes=56 * 2 ** 20
            ),
            cost_estimate=pl.CostEstimate(
                flops=units * 4 * tok * tok * DH,
                bytes_accessed=8 * query.size,
                transcendentals=units * tok * tok,
            ),
        )(pair_keys, pair_count, query, keys_in, values_in)

    tokens = P("ctx", "head", None)
    return jax.shard_map(
        body,
        mesh=mesh,
        in_specs=(tokens, tokens, tokens, P("ctx", None), P("ctx")),
        out_specs=tokens,
        check_vma=False,
    )
```

time: 116 us -> 114 us (0.983)
  the two profiles are of different devices: /device:TPU:2 before, /device:TPU:122 now
where the time goes in v3:
time: 114 us
  Pallas kernels  110 us (96%)
  local copies, waits for them, and re-layouts  3.22 us (3%)
    pallas_call x1, Pallas kernels, body(): pl.pallas_call(build_kernel(n_head, n_ctx, tiles, rows, heads, most), out...  110 us
    unnamed x1, local copies, waits for them, and re-layouts  3.22 us

profile of v3, /device:TPU:122, one launch (start us, length us, event | category | flops | bytes accessed | tf_op | source)
XLA Modules:
  0.0 113.6 jit_solution(11577329624539617900)
XLA Ops:
  0.0 110.4 %shard_map.55 = bf16[4,96,3072]{2,1,0:T(8,128)(2,1)} custom-call(s32[4,8]{1,0:T(4,128)} %slots_ref.1, s32[4]{0:T(128)} %count_ref.1, bf16[4,96,3072]{2,1,0:T(8,128)(2,1)} %q_ref.1, bf16[4,96,3072]{2,1,0:T(8,128)(2,1)} %k_ref.1, bf16[4,96,3072]{2,1,0:T(8,128)(2,1)} %v_ref.1), custom_call_target="tpu_custom_call" | custom-call | flops 14495514624 | bytes 9437184 | tf_op jit(solution)/shard_map/pallas_call | solution.py:225
  110.4 3.2 %copy.7 = bf16[4,96,3072]{2,1,0:T(8,128)(2,1)} copy(bf16[4,96,3072]{2,1,0:T(8,128)(2,1)} %shard_map.55) | data formatting | bytes 4718592

commit v4 on v3

--- a/solution.py
+++ b/solution.py
@@ -18,7 +18,9 @@
 
     def kernel(slots_ref, count_ref, q_ref, k_ref, v_ref, out_ref, *scratch):
         kwin, vwin = scratch[:heads], scratch[heads:2 * heads]
-        q_all, k_all, o_all, rx, tx, win, wtx, o_rx, o_tx = scratch[2 * heads:]
+        q_all, k_all, o_all, *rest = scratch[2 * heads:]
+        score_bufs, tops = rest[:2], rest[2:4]
+        rx, tx, win, wtx, o_rx, o_tx = rest[4:]
         me_h, me_c = lax.axis_index("head"), lax.axis_index("ctx")
         first_slot = (me_c - 1) * tiles
         others = [lax.rem(me_h + step, n_head) for step in (1, n_head - 1, *range(2, n_head - 1))]
@@ -105,43 +107,66 @@
 
             lax.fori_loop(0, tiles, pass_on, 0)
 
-        def compute(g, duties):
-            def one_tile(t, carry):
-                query = q_all[g, t]
-                live = count_ref[t]
-                shifts = [jnp.where(p < live, 0.0, MASKED).astype(jnp.float32) for p in range(most)]
-                slots = [jnp.clip(slots_ref[t, p] - first_slot, 0, 3 * tiles - 1) for p in range(most)]
-                scores, top = [], jnp.full((tok, DH), -MASKED, jnp.float32)
-                for p in range(0, most, 2):
-                    keys = jnp.concatenate([kwin[g][slots[p]], kwin[g][slots[p + 1]]], axis=1)
+        half = tok // 2
+
+        def pair_of(t, p):
+            slot = jnp.clip(slots_ref[t, p] - first_slot, 0, 3 * tiles - 1)
+            return slot, jnp.where(p < count_ref[t], 0.0, MASKED).astype(jnp.float32)
+
+        def half_step(g, done, coming):
+            if coming is not None:
+                t_in, side_in = coming
+                query = q_all[g, t_in, side_in * half:(side_in + 1) * half]
+                top_in = jnp.full((half, DH), -MASKED, jnp.float32)
+            if done is not None:
+                t_out, side_out = done
+                top_out = tops[side_out][...]
+                merged = jnp.zeros((half, 2 * DH), jnp.float32)
+                ones = jnp.ones((2 * tok, DH), jnp.bfloat16)
+            for p in range(0, most, 2):
+                if coming is not None:
+                    (slot0, shift0), (slot1, shift1) = pair_of(t_in, p), pair_of(t_in, p + 1)
+                    keys = jnp.concatenate([kwin[g][slot0], kwin[g][slot1]], axis=1)
                     both = jnp.dot(query, keys, preferred_element_type=jnp.float32)
-                    for s, shift in zip((both[:, :tok], both[:, tok:]), shifts[p:p + 2]):
-                        most_of = s[:, :DH]
-                        for at in range(DH, tok, DH):
-                            most_of = jnp.maximum(most_of, s[:, at:at + DH])
-                        top = jnp.maximum(top, most_of - shift)
-                        scores.append(s)
-                top = jnp.max(top, axis=1, keepdims=True) * EXP2_SCALE
-                ones = jnp.ones((2 * tok, DH), jnp.bfloat16)
-                merged = jnp.zeros((tok, 2 * DH), jnp.float32)
-                for p in range(0, most, 2):
-                    weights = [
-                        jnp.exp2(s * EXP2_SCALE - (top + shift)).astype(jnp.bfloat16)
-                        for s, shift in zip(scores[p:p + 2], shifts[p:p + 2])
-                    ]
-                    values = jnp.concatenate([vwin[g][slots[p]], vwin[g][slots[p + 1]]], axis=0)
+                    score_bufs[side_in][:, p * tok:(p + 2) * tok] = both
+                    for start, shift in ((0, shift0), (tok, shift1)):
+                        most_of = both[:, start:start + DH]
+                        for at in range(start + DH, start + tok, DH):
+                            most_of = jnp.maximum(most_of, both[:, at:at + DH])
+                        top_in = jnp.maximum(top_in, most_of - shift)
+                if done is not None:
+                    (slot0, shift0), (slot1, shift1) = pair_of(t_out, p), pair_of(t_out, p + 1)
+                    weights = []
+                    for start, shift in ((p * tok, shift0), ((p + 1) * tok, shift1)):
+                        base = top_out + shift
+                        for at in range(start, start + tok, DH):
+                            s = score_bufs[side_out][:, at:at + DH]
+                            weights.append(jnp.exp2(s * EXP2_SCALE - base).astype(jnp.bfloat16))
+                    values = jnp.concatenate([vwin[g][slot0], vwin[g][slot1]], axis=0)
                     merged = merged + jnp.dot(
                         jnp.concatenate(weights, axis=1),
                         jnp.concatenate([values, ones], axis=1),
                         preferred_element_type=jnp.float32,
                     )
-                o_all[g, t] = (merged[:, :DH] / merged[:, DH:]).astype(jnp.bfloat16)
+            if coming is not None:
+                top_in = jnp.max(top_in, axis=1, keepdims=True) * EXP2_SCALE
+                tops[side_in][...] = jnp.broadcast_to(top_in, (half, DH))
+            if done is not None:
+                o_all[g, t_out, side_out * half:(side_out + 1) * half] = (
+                    merged[:, :DH] / merged[:, DH:]
+                ).astype(jnp.bfloat16)
+
+        def compute(g, duties):
+            def one_tile(t, carry):
+                half_step(g, (t, 0), (t, 1))
+                half_step(g, (t, 1), (jnp.minimum(t + 1, tiles - 1), 0))
                 if g == heads - 1:
                     send_output(g, t)
                 for at, duty in duties:
                     pl.when(t == at)(duty)
                 return carry
 
+            half_step(g, None, (0, 0))
             lax.fori_loop(0, tiles, one_tile, 0)
 
         def send_output(g, t):
@@ -219,17 +244,19 @@
         scratch = [pltpu.VMEM((3 * tiles, DH, tok), jnp.bfloat16)] * heads
         scratch += [pltpu.VMEM((3 * tiles, tok, DH), jnp.bfloat16)] * heads
         scratch += [pltpu.VMEM((heads, tiles, tok, DH), jnp.bfloat16)] * 3
+        scratch += [pltpu.VMEM((tok // 2, most * tok), jnp.float32)] * 2
+        scratch += [pltpu.VMEM((tok // 2, DH), jnp.float32)] * 2
         scratch += [dma((3, heads)), dma((3,)), dma((2, heads)), dma((2, 2, heads)), dma((heads,)), dma((heads,))]
         smem = pl.BlockSpec(memory_space=pltpu.SMEM)
-        anywhere = pl.BlockSpec(memory_space=pl.ANY)
+        in_hbm = pl.BlockSpec(memory_space=pltpu.HBM)
         return pl.pallas_call(
             build_kernel(n_head, n_ctx, tiles, rows, heads, most),
-            out_shape=jax.ShapeDtypeStruct(query.shape, query.dtype),
-            in_specs=[smem, smem, anywhere, anywhere, anywhere],
-            out_specs=anywhere,
+            out_shape=pltpu.VMEM(query.shape, query.dtype),
+            in_specs=[smem, smem, in_hbm, in_hbm, in_hbm],
+            out_specs=pl.BlockSpec(memory_space=pltpu.VMEM),
             scratch_shapes=scratch,
             compiler_params=pltpu.CompilerParams(
-                collective_id=0, has_side_effects=True, vmem_limit_bytes=56 * 2 ** 20
+                collective_id=0, has_side_effects=True, vmem_limit_bytes=60 * 2 ** 20
             ),
             cost_estimate=pl.CostEstimate(
                 flops=units * 4 * tok * tok * DH,

time: 114 us -> 111 us (0.974)
  local copies, waits for them, and re-layouts: 3.22 us -> 1.41 us
    unnamed x1, local copies, waits for them, and re-layouts: 3.22 us -> 1.41 us
where the time goes in v4:
time: 111 us
  Pallas kernels  109 us (98%)
  local copies, waits for them, and re-layouts  1.41 us (1%)
    pallas_call x1, Pallas kernels, body(): pl.pallas_call(build_kernel(n_head, n_ctx, tiles, rows, heads, most), out...  109 us

profile of v4, /device:TPU:122, one launch (start us, length us, event | category | flops | bytes accessed | tf_op | source)
XLA Modules:
  0.0 110.8 jit_solution(3047901917461086280)
XLA Ops:
  0.0 109.4 %shard_map.55 = bf16[4,96,3072]{2,1,0:T(8,128)(2,1)S(1)} custom-call(s32[4,8]{1,0:T(4,128)} %slots_ref.1, s32[4]{0:T(128)} %count_ref.1, bf16[4,96,3072]{2,1,0:T(8,128)(2,1)} %q_ref.1, bf16[4,96,3072]{2,1,0:T(8,128)(2,1)} %k_ref.1, bf16[4,96,3072]{2,1,0:T(8,128)(2,1)} %v_ref.1), custom_call_target="tpu_custom_call" | custom-call | flops 14495514624 | bytes 9437184 | tf_op jit(solution)/shard_map/pallas_call | solution.py:252
  109.4 1.4 %copy.7 = bf16[4,96,3072]{2,1,0:T(8,128)(2,1)} copy(bf16[4,96,3072]{2,1,0:T(8,128)(2,1)S(1)} %shard_map.55) | data formatting | bytes 4718592

commit v5 on v4

--- a/solution.py
+++ b/solution.py
@@ -16,11 +16,12 @@
 def build_kernel(n_head, n_ctx, tiles, rows, heads, most):
     tok = n_head * rows
 
-    def kernel(slots_ref, count_ref, q_ref, k_ref, v_ref, out_ref, *scratch):
+    def kernel(slots_hbm, count_hbm, q_ref, k_ref, v_ref, out_ref, *scratch):
         kwin, vwin = scratch[:heads], scratch[heads:2 * heads]
         q_all, k_all, o_all, *rest = scratch[2 * heads:]
         score_bufs, tops = rest[:2], rest[2:4]
-        rx, tx, win, wtx, o_rx, o_tx = rest[4:]
+        slots_ref, count_ref = rest[4:6]
+        rx, tx, win, wtx, o_rx, o_tx, lists = rest[6:]
         me_h, me_c = lax.axis_index("head"), lax.axis_index("ctx")
         first_slot = (me_c - 1) * tiles
         others = [lax.rem(me_h + step, n_head) for step in (1, n_head - 1, *range(2, n_head - 1))]
@@ -61,8 +62,11 @@
                         device_id={"head": other},
                         device_id_type=MESH,
                     ).start()
+            for which in kinds:
                 pltpu.make_async_copy(
-                    source.at[:, :, head_columns(me_h, g)], target, rx.at[which, g]
+                    (k_ref, v_ref, q_ref)[which].at[:, :, head_columns(me_h, g)],
+                    landing(which, g).at[:, token_rows(me_h), :],
+                    rx.at[which, g],
                 ).start()
 
         def await_bytes(ref, sem):
@@ -169,11 +173,11 @@
             half_step(g, None, (0, 0))
             lax.fori_loop(0, tiles, one_tile, 0)
 
-        def send_output(g, t):
-            target = out_ref.at[t, :, head_columns(me_h, g)]
+        def send_output(g, ts):
+            target = out_ref.at[ts, :, head_columns(me_h, g)]
             for other in others:
                 pltpu.make_async_remote_copy(
-                    src_ref=o_all.at[g, t, token_rows(other), :],
+                    src_ref=o_all.at[g, ts, token_rows(other), :],
                     dst_ref=target,
                     send_sem=o_tx.at[g],
                     recv_sem=o_rx.at[g],
@@ -181,25 +185,29 @@
                     device_id_type=MESH,
                 ).start()
             pltpu.make_async_copy(
-                o_all.at[g, t, token_rows(me_h), :], target, o_rx.at[g]
+                o_all.at[g, ts, token_rows(me_h), :], target, o_rx.at[g]
             ).start()
 
         def send_outputs(g):
-            def one_tile(t, carry):
-                send_output(g, t)
-                return carry
-
-            lax.fori_loop(0, tiles, one_tile, 0)
+            send_output(g, slice(None))
 
         def later(duty, *args):
             return functools.partial(duty, *args) if args[-1] < heads else lambda: None
 
         send_inputs((0, 1, 2), 0)
         later(send_inputs, (0, 1), 1)()
+        list_copies = [
+            pltpu.make_async_copy(source, target, lists.at[i])
+            for i, (source, target) in enumerate(((slots_hbm, slots_ref), (count_hbm, count_ref)))
+        ]
+        for copy in list_copies:
+            copy.start()
         share_keys(0)
         share_values(0)
         later(send_inputs, (2,), 1)()
         later(send_inputs, (0, 1), 2)()
+        for copy in list_copies:
+            copy.wait()
         for g in range(heads):
             duties = [(0, later(send_inputs, (0, 1), g + 3)), (0, later(send_inputs, (2,), g + 2))]
             sharing = [(0, later(share_keys, g + 1)), (1, later(share_values, g + 1))]
@@ -246,13 +254,13 @@
         scratch += [pltpu.VMEM((heads, tiles, tok, DH), jnp.bfloat16)] * 3
         scratch += [pltpu.VMEM((tok // 2, most * tok), jnp.float32)] * 2
         scratch += [pltpu.VMEM((tok // 2, DH), jnp.float32)] * 2
-        scratch += [dma((3, heads)), dma((3,)), dma((2, heads)), dma((2, 2, heads)), dma((heads,)), dma((heads,))]
-        smem = pl.BlockSpec(memory_space=pltpu.SMEM)
+        scratch += [pltpu.SMEM(pair_keys.shape, jnp.int32), pltpu.SMEM(pair_count.shape, jnp.int32)]
+        scratch += [dma((3, heads)), dma((3,)), dma((2, heads)), dma((2, 2, heads)), dma((heads,)), dma((heads,)), dma((2,))]
         in_hbm = pl.BlockSpec(memory_space=pltpu.HBM)
         return pl.pallas_call(
             build_kernel(n_head, n_ctx, tiles, rows, heads, most),
             out_shape=pltpu.VMEM(query.shape, query.dtype),
-            in_specs=[smem, smem, in_hbm, in_hbm, in_hbm],
+            in_specs=[in_hbm] * 5,
             out_specs=pl.BlockSpec(memory_space=pltpu.VMEM),
             scratch_shapes=scratch,
             compiler_params=pltpu.CompilerParams(

time: 111 us -> 110 us (level)
  no operation moved by 1% of the time
where the time goes in v5:
time: 110 us
  Pallas kernels  109 us (99%)
  local copies, waits for them, and re-layouts  1.41 us (1%)
    pallas_call x1, Pallas kernels, body(): pl.pallas_call(build_kernel(n_head, n_ctx, tiles, rows, heads, most), out...  109 us

profile of v5, /device:TPU:122, one launch (start us, length us, event | category | flops | bytes accessed | tf_op | source)
XLA Modules:
  0.0 110.3 jit_solution(13317247724471036846)
XLA Ops:
  0.0 108.9 %shard_map.55 = bf16[4,96,3072]{2,1,0:T(8,128)(2,1)S(1)} custom-call(s32[4,8]{1,0:T(4,128)} %slots_hbm.1, s32[4]{0:T(128)} %count_hbm.1, bf16[4,96,3072]{2,1,0:T(8,128)(2,1)} %q_ref.1, bf16[4,96,3072]{2,1,0:T(8,128)(2,1)} %k_ref.1, bf16[4,96,3072]{2,1,0:T(8,128)(2,1)} %v_ref.1), custom_call_target="tpu_custom_call" | custom-call | flops 14495514624 | bytes 9437184 | tf_op jit(solution)/shard_map/pallas_call | solution.py:260
  108.9 1.4 %copy.7 = bf16[4,96,3072]{2,1,0:T(8,128)(2,1)} copy(bf16[4,96,3072]{2,1,0:T(8,128)(2,1)S(1)} %shard_map.55) | data formatting | bytes 4718592

commit v6 on v5

--- a/solution.py
+++ b/solution.py
@@ -111,21 +111,19 @@
 
             lax.fori_loop(0, tiles, pass_on, 0)
 
-        half = tok // 2
-
         def pair_of(t, p):
             slot = jnp.clip(slots_ref[t, p] - first_slot, 0, 3 * tiles - 1)
             return slot, jnp.where(p < count_ref[t], 0.0, MASKED).astype(jnp.float32)
 
-        def half_step(g, done, coming):
+        def step(g, done, coming):
             if coming is not None:
                 t_in, side_in = coming
-                query = q_all[g, t_in, side_in * half:(side_in + 1) * half]
-                top_in = jnp.full((half, DH), -MASKED, jnp.float32)
+                query = q_all[g, t_in]
+                top_in = jnp.full((tok, DH), -MASKED, jnp.float32)
             if done is not None:
                 t_out, side_out = done
                 top_out = tops[side_out][...]
-                merged = jnp.zeros((half, 2 * DH), jnp.float32)
+                merged = jnp.zeros((tok, 2 * DH), jnp.float32)
                 ones = jnp.ones((2 * tok, DH), jnp.bfloat16)
             for p in range(0, most, 2):
                 if coming is not None:
@@ -154,24 +152,30 @@
                     )
             if coming is not None:
                 top_in = jnp.max(top_in, axis=1, keepdims=True) * EXP2_SCALE
-                tops[side_in][...] = jnp.broadcast_to(top_in, (half, DH))
+                tops[side_in][...] = jnp.broadcast_to(top_in, (tok, DH))
             if done is not None:
-                o_all[g, t_out, side_out * half:(side_out + 1) * half] = (
-                    merged[:, :DH] / merged[:, DH:]
-                ).astype(jnp.bfloat16)
+                o_all[g, t_out] = (merged[:, :DH] / merged[:, DH:]).astype(jnp.bfloat16)
 
         def compute(g, duties):
-            def one_tile(t, carry):
-                half_step(g, (t, 0), (t, 1))
-                half_step(g, (t, 1), (jnp.minimum(t + 1, tiles - 1), 0))
+            def finish(t):
                 if g == heads - 1:
                     send_output(g, t)
                 for at, duty in duties:
                     pl.when(t == at)(duty)
+
+            def two_tiles(i, carry):
+                step(g, (2 * i, 0), (2 * i + 1, 1))
+                finish(2 * i)
+                last = i == tiles // 2 - 1
+                pl.when(last)(functools.partial(step, g, (2 * i + 1, 1), None))
+                pl.when(jnp.logical_not(last))(
+                    functools.partial(step, g, (2 * i + 1, 1), (jnp.minimum(2 * i + 2, tiles - 1), 0))
+                )
+                finish(2 * i + 1)
                 return carry
 
-            half_step(g, None, (0, 0))
-            lax.fori_loop(0, tiles, one_tile, 0)
+            step(g, None, (0, 0))
+            lax.fori_loop(0, tiles // 2, two_tiles, 0)
 
         def send_output(g, ts):
             target = out_ref.at[ts, :, head_columns(me_h, g)]
@@ -252,8 +256,8 @@
         scratch = [pltpu.VMEM((3 * tiles, DH, tok), jnp.bfloat16)] * heads
         scratch += [pltpu.VMEM((3 * tiles, tok, DH), jnp.bfloat16)] * heads
         scratch += [pltpu.VMEM((heads, tiles, tok, DH), jnp.bfloat16)] * 3
-        scratch += [pltpu.VMEM((tok // 2, most * tok), jnp.float32)] * 2
-        scratch += [pltpu.VMEM((tok // 2, DH), jnp.float32)] * 2
+        scratch += [pltpu.VMEM((tok, most * tok), jnp.float32)] * 2
+        scratch += [pltpu.VMEM((tok, DH), jnp.float32)] * 2
         scratch += [pltpu.SMEM(pair_keys.shape, jnp.int32), pltpu.SMEM(pair_count.shape, jnp.int32)]
         scratch += [dma((3, heads)), dma((3,)), dma((2, heads)), dma((2, 2, heads)), dma((heads,)), dma((heads,)), dma((2,))]
         in_hbm = pl.BlockSpec(memory_space=pltpu.HBM)

time: 110 us -> 111 us (level)
  no operation moved by 1% of the time
where the time goes in v6:
time: 111 us
  Pallas kernels  109 us (98%)
  local copies, waits for them, and re-layouts  1.41 us (1%)
    pallas_call x1, Pallas kernels, body(): pl.pallas_call(build_kernel(n_head, n_ctx, tiles, rows, heads, most), out...  109 us

profile of v6, /device:TPU:122, one launch (start us, length us, event | category | flops | bytes accessed | tf_op | source)
XLA Modules:
  0.0 110.6 jit_solution(2688171735955705376)
XLA Ops:
  0.0 109.2 %shard_map.55 = bf16[4,96,3072]{2,1,0:T(8,128)(2,1)S(1)} custom-call(s32[4,8]{1,0:T(4,128)} %slots_hbm.1, s32[4]{0:T(128)} %count_hbm.1, bf16[4,96,3072]{2,1,0:T(8,128)(2,1)} %q_ref.1, bf16[4,96,3072]{2,1,0:T(8,128)(2,1)} %k_ref.1, bf16[4,96,3072]{2,1,0:T(8,128)(2,1)} %v_ref.1), custom_call_target="tpu_custom_call" | custom-call | flops 14495514624 | bytes 9437184 | tf_op jit(solution)/shard_map/pallas_call | solution.py:264
  109.2 1.4 %copy.7 = bf16[4,96,3072]{2,1,0:T(8,128)(2,1)} copy(bf16[4,96,3072]{2,1,0:T(8,128)(2,1)S(1)} %shard_map.55) | data formatting | bytes 4718592

commit v7 on v5

--- a/solution.py
+++ b/solution.py
@@ -19,6 +19,7 @@
     def kernel(slots_hbm, count_hbm, q_ref, k_ref, v_ref, out_ref, *scratch):
         kwin, vwin = scratch[:heads], scratch[heads:2 * heads]
         q_all, k_all, o_all, *rest = scratch[2 * heads:]
+        staged, staging = rest.pop(), rest.pop()
         score_bufs, tops = rest[:2], rest[2:4]
         slots_ref, count_ref = rest[4:6]
         rx, tx, win, wtx, o_rx, o_tx, lists = rest[6:]
@@ -26,6 +27,12 @@
         first_slot = (me_c - 1) * tiles
         others = [lax.rem(me_h + step, n_head) for step in (1, n_head - 1, *range(2, n_head - 1))]
 
+        stage_copies = [
+            pltpu.make_async_copy(source, staged.at[which], staging.at[which])
+            for which, source in enumerate((k_ref, v_ref, q_ref))
+        ]
+        for copy in stage_copies:
+            copy.start()
         barrier = pltpu.get_barrier_semaphore()
         for other in others:
             pl.semaphore_signal(barrier, inc=1, device_id={"head": other}, device_id_type=MESH)
@@ -51,7 +58,7 @@
 
         def send_inputs(kinds, g):
             for which in kinds:
-                source = (k_ref, v_ref, q_ref)[which]
+                source = staged.at[which] if g > 0 else (k_ref, v_ref, q_ref)[which]
                 target = landing(which, g).at[:, token_rows(me_h), :]
                 for other in others:
                     pltpu.make_async_remote_copy(
@@ -64,7 +71,7 @@
                     ).start()
             for which in kinds:
                 pltpu.make_async_copy(
-                    (k_ref, v_ref, q_ref)[which].at[:, :, head_columns(me_h, g)],
+                    (staged.at[which] if g > 0 else (k_ref, v_ref, q_ref)[which]).at[:, :, head_columns(me_h, g)],
                     landing(which, g).at[:, token_rows(me_h), :],
                     rx.at[which, g],
                 ).start()
@@ -195,6 +202,8 @@
             return functools.partial(duty, *args) if args[-1] < heads else lambda: None
 
         send_inputs((0, 1, 2), 0)
+        for copy in stage_copies:
+            copy.wait()
         later(send_inputs, (0, 1), 1)()
         list_copies = [
             pltpu.make_async_copy(source, target, lists.at[i])
@@ -256,6 +265,7 @@
         scratch += [pltpu.VMEM((tok // 2, DH), jnp.float32)] * 2
         scratch += [pltpu.SMEM(pair_keys.shape, jnp.int32), pltpu.SMEM(pair_count.shape, jnp.int32)]
         scratch += [dma((3, heads)), dma((3,)), dma((2, heads)), dma((2, 2, heads)), dma((heads,)), dma((heads,)), dma((2,))]
+        scratch += [dma((3,)), pltpu.VMEM((3, *query.shape), jnp.bfloat16)]
         in_hbm = pl.BlockSpec(memory_space=pltpu.HBM)
         return pl.pallas_call(
             build_kernel(n_head, n_ctx, tiles, rows, heads, most),

time: 110 us -> 110 us (level)
  no operation moved by 1% of the time
where the time goes in v7:
time: 110 us
  Pallas kernels  109 us (99%)
  local copies, waits for them, and re-layouts  1.41 us (1%)
    pallas_call x1, Pallas kernels, body(): pl.pallas_call(build_kernel(n_head, n_ctx, tiles, rows, heads, most), out...  109 us

profile of v7, /device:TPU:122, one launch (start us, length us, event | category | flops | bytes accessed | tf_op | source)
XLA Modules:
  0.0 110.3 jit_solution(7511429113067245957)
XLA Ops:
  0.0 108.9 %shard_map.55 = bf16[4,96,3072]{2,1,0:T(8,128)(2,1)S(1)} custom-call(s32[4,8]{1,0:T(4,128)} %slots_hbm.1, s32[4]{0:T(128)} %count_hbm.1, bf16[4,96,3072]{2,1,0:T(8,128)(2,1)} %q_ref.1, bf16[4,96,3072]{2,1,0:T(8,128)(2,1)} %k_ref.1, bf16[4,96,3072]{2,1,0:T(8,128)(2,1)} %v_ref.1), custom_call_target="tpu_custom_call" | custom-call | flops 14495514624 | bytes 9437184 | tf_op jit(solution)/shard_map/pallas_call | solution.py:270
  108.9 1.4 %copy.7 = bf16[4,96,3072]{2,1,0:T(8,128)(2,1)} copy(bf16[4,96,3072]{2,1,0:T(8,128)(2,1)S(1)} %shard_map.55) | data formatting | bytes 4718592

commit v8 on v5

--- a/solution.py
+++ b/solution.py
@@ -24,7 +24,7 @@
         rx, tx, win, wtx, o_rx, o_tx, lists = rest[6:]
         me_h, me_c = lax.axis_index("head"), lax.axis_index("ctx")
         first_slot = (me_c - 1) * tiles
-        others = [lax.rem(me_h + step, n_head) for step in (1, n_head - 1, *range(2, n_head - 1))]
+        others = [lax.rem(me_h + step, n_head) for step in (*range(2, n_head - 1), 1, n_head - 1)]
 
         barrier = pltpu.get_barrier_semaphore()
         for other in others:

time: 110 us -> 110 us (level)
  no operation moved by 1% of the time
where the time goes in v8:
time: 110 us
  Pallas kernels  108 us (98%)
  local copies, waits for them, and re-layouts  1.41 us (1%)
    pallas_call x1, Pallas kernels, body(): pl.pallas_call(build_kernel(n_head, n_ctx, tiles, rows, heads, most), out...  108 us

profile of v8, /device:TPU:122, one launch (start us, length us, event | category | flops | bytes accessed | tf_op | source)
XLA Modules:
  0.0 109.6 jit_solution(8004229079018458985)
XLA Ops:
  0.0 108.2 %shard_map.55 = bf16[4,96,3072]{2,1,0:T(8,128)(2,1)S(1)} custom-call(s32[4,8]{1,0:T(4,128)} %slots_hbm.1, s32[4]{0:T(128)} %count_hbm.1, bf16[4,96,3072]{2,1,0:T(8,128)(2,1)} %q_ref.1, bf16[4,96,3072]{2,1,0:T(8,128)(2,1)} %k_ref.1, bf16[4,96,3072]{2,1,0:T(8,128)(2,1)} %v_ref.1), custom_call_target="tpu_custom_call" | custom-call | flops 14495514624 | bytes 9437184 | tf_op jit(solution)/shard_map/pallas_call | solution.py:260
  108.2 1.4 %copy.7 = bf16[4,96,3072]{2,1,0:T(8,128)(2,1)} copy(bf16[4,96,3072]{2,1,0:T(8,128)(2,1)S(1)} %shard_map.55) | data formatting | bytes 4718592

commit v9 on v8

--- a/solution.py
+++ b/solution.py
@@ -72,14 +72,14 @@
         def await_bytes(ref, sem):
             pltpu.make_async_copy(ref, ref, sem).wait()
 
-        def send_window(which, window, g, t):
-            own = window[g].at[tiles + t]
+        def send_window(which, window, g, t, count=1):
+            own = window[g].at[pl.ds(tiles + t, count)]
             for side, (other, inside) in enumerate(ctx_sides):
                 @pl.when(inside)
                 def _():
                     pltpu.make_async_remote_copy(
                         src_ref=own,
-                        dst_ref=window[g].at[2 * tiles * side + t],
+                        dst_ref=window[g].at[pl.ds(2 * tiles * side + t, count)],
                         send_sem=wtx.at[which, side, g],
                         recv_sem=win.at[which, g],
                         device_id={"ctx": other},
@@ -89,7 +89,7 @@
                 @pl.when(jnp.logical_not(inside))
                 def _():
                     pltpu.make_async_copy(
-                        own, window[g].at[2 * tiles * (1 - side) + t], win.at[which, g]
+                        own, window[g].at[pl.ds(2 * tiles * (1 - side) + t, count)], win.at[which, g]
                     ).start()
 
         def share_keys(g):
@@ -104,12 +104,7 @@
 
         def share_values(g):
             await_bytes(landing(1, g), rx.at[1, g])
-
-            def pass_on(t, carry):
-                send_window(1, vwin, g, t)
-                return carry
-
-            lax.fori_loop(0, tiles, pass_on, 0)
+            send_window(1, vwin, g, 0, tiles)
 
         half = tok // 2
 

time: 110 us -> 110 us (level)
  no operation moved by 1% of the time
where the time goes in v9:
time: 110 us
  Pallas kernels  108 us (98%)
  local copies, waits for them, and re-layouts  1.41 us (1%)
    pallas_call x1, Pallas kernels, body(): pl.pallas_call(build_kernel(n_head, n_ctx, tiles, rows, heads, most), out...  108 us

profile of v9, /device:TPU:122, one launch (start us, length us, event | category | flops | bytes accessed | tf_op | source)
XLA Modules:
  0.0 109.6 jit_solution(14175044556745027742)
XLA Ops:
  0.0 108.2 %shard_map.55 = bf16[4,96,3072]{2,1,0:T(8,128)(2,1)S(1)} custom-call(s32[4,8]{1,0:T(4,128)} %slots_hbm.1, s32[4]{0:T(128)} %count_hbm.1, bf16[4,96,3072]{2,1,0:T(8,128)(2,1)} %q_ref.1, bf16[4,96,3072]{2,1,0:T(8,128)(2,1)} %k_ref.1, bf16[4,96,3072]{2,1,0:T(8,128)(2,1)} %v_ref.1), custom_call_target="tpu_custom_call" | custom-call | flops 14495514624 | bytes 9437184 | tf_op jit(solution)/shard_map/pallas_call | solution.py:255
  108.2 1.4 %copy.7 = bf16[4,96,3072]{2,1,0:T(8,128)(2,1)} copy(bf16[4,96,3072]{2,1,0:T(8,128)(2,1)S(1)} %shard_map.55) | data formatting | bytes 4718592
